TPU v7x, 128 devices: a whole 4x4x4 slice. The times are simulated.
128 devices in a mesh: seq: 16 (over z, y), tp: 8 (over x, core).
Axes of the slice: x: 4, y: 4, z: 4, core: 2. Of those that a mesh axis runs over, the one named last changes fastest.
Arguments:
- queries: bfloat16 [8192, 4096], P('seq', 'tp'), may hold values from -8 to 8
- nb_keys: bfloat16 [32768, 4096], P('seq', 'tp'), may hold values from -8 to 8
- nb_values: bfloat16 [32768, 4096], P('seq', 'tp'), may hold values from -6 to 6
- out_weight: bfloat16 [4096, 8192], P('tp'), may hold values from -0.09375 to 0.09375
- out_grad: bfloat16 [8192, 8192], P(('seq', 'tp')), may hold values from -6 to 6
- span_refs: int32 [128, 2], P('seq'), may hold values from 0 to 31, as said below
- block_dest: int32 [256], P('seq'), may hold values from 0 to 15, as said below
- block_valid: int32 [256], P('seq'), may hold values from 32 to 128, as said below
Outputs:
- mixed: bfloat16 [8192, 8192], P(('seq', 'tp'))
- d_queries: bfloat16 [8192, 4096], P('seq', 'tp')
- d_keys: bfloat16 [32768, 4096], P('seq', 'tp')
- d_values: bfloat16 [32768, 4096], P('seq', 'tp')
Inputs may be any that keep to these rules, and one draw needn't show every extreme that they name: `block_dest`: each index of seq sends its blocks to 8 distinct owners, exactly 2 blocks to each; one of them is its own index, and 4 owners drawn afresh receive 2 blocks from every index. `span_refs`: the two slots of a span differ, and each holds a block sent to that span's owner: slot s * 2 + c holds the block of rank c that index s sends there. `block_valid`: the first block of every index of seq has all 128 rows valid.
All inputs are finite; a program needn't handle non-finite values.
Results may differ from a plain program's by a relative error of at most 0.017.
Values may be sent and summed in bfloat16 or wider, within the bound.
No kernel may reach another device: no remote copies, remote signals or barrier semaphores. Data moves between devices by JAX's collectives and lax.ppermute only.
A program may use at most 128 MiB of HBM per device.

v0:
```python
import jax
import jax.numpy as jnp
from jax import lax
from jax.sharding import PartitionSpec as P

HD = 128
SPAN = 64
BR = 128
NEIGH = 2
CAP = 2


def on_device(
    queries, nb_keys, nb_values, out_weight, out_grad, span_refs, block_dest, block_valid
):
    seq_count = lax.axis_size("seq")
    tp_count = lax.axis_size("tp")
    col_width = queries.shape[1]
    heads_here = col_width // HD
    tokens_here = queries.shape[0]
    local_span_list = tokens_here // SPAN
    blocks_here = block_dest.shape[0]
    slot_count = seq_count * CAP
    rows_out = tokens_here // tp_count
    score_scale = HD ** (-0.5)
    same_owner = block_dest[:, None] == block_dest[None, :]
    before = jnp.arange(blocks_here)[:, None] < jnp.arange(blocks_here)[None, :]
    slot_rank = jnp.sum((same_owner & before).astype(jnp.int32), axis=0)
    target = block_dest * CAP + slot_rank
    select = (target[None, :] == jnp.arange(slot_count)[:, None]).astype(jnp.bfloat16)

    def pack(block_rows):
        packed = jnp.dot(
            select,
            block_rows.reshape(blocks_here, BR * col_width),
            preferred_element_type=jnp.float32,
        )
        return packed.astype(jnp.bfloat16).reshape(seq_count, CAP, BR * col_width)

    sent_valid = jnp.dot(
        select.astype(jnp.float32), block_valid.astype(jnp.float32), precision=lax.Precision.HIGHEST
    )
    sent_valid = sent_valid.astype(jnp.bfloat16).reshape(seq_count, CAP)
    recv_keys, recv_values, recv_valid = (
        lax.all_to_all(pack(nb_keys), "seq", split_axis=0, concat_axis=0, tiled=True),
        lax.all_to_all(pack(nb_values), "seq", split_axis=0, concat_axis=0, tiled=True),
        lax.all_to_all(sent_valid, "seq", split_axis=0, concat_axis=0, tiled=True),
    )
    recv_keys = recv_keys.reshape(slot_count, BR * col_width)
    recv_values = recv_values.reshape(slot_count, BR * col_width)
    recv_valid = recv_valid.reshape(slot_count)
    span_slots = span_refs.reshape(-1)
    key_rows = jnp.take(recv_keys, span_slots, axis=0).reshape(
        local_span_list, NEIGH * BR, heads_here, HD
    )
    value_rows = jnp.take(recv_values, span_slots, axis=0).reshape(
        local_span_list, NEIGH * BR, heads_here, HD
    )
    valid_rows = (
        jnp.take(recv_valid, span_slots).astype(jnp.float32).reshape(local_span_list, NEIGH)
    )
    row_pos = jnp.arange(BR).astype(jnp.float32)
    live_keys = (row_pos[None, None, :] < valid_rows[:, :, None]).reshape(
        local_span_list, NEIGH * BR
    )
    live_mask = live_keys[:, None, None, :]
    query_rows = queries.reshape(local_span_list, SPAN, heads_here, HD)
    scores = (
        jnp.einsum("cqhd,ckhd->chqk", query_rows, key_rows, preferred_element_type=jnp.float32)
        * score_scale
    )
    masked = jnp.where(live_mask, scores, -1e30)
    row_max = jnp.max(masked, axis=-1, keepdims=True)
    exp_terms = jnp.where(live_mask, jnp.exp(masked - row_max), 0.0)
    attn_prob = exp_terms / jnp.sum(exp_terms, axis=-1, keepdims=True)
    prob_b = attn_prob.astype(jnp.bfloat16)
    attended = jnp.einsum("chqk,ckhd->cqhd", prob_b, value_rows, preferred_element_type=jnp.float32)
    attended = attended.astype(jnp.bfloat16).reshape(tokens_here, col_width)
    summed = lax.psum(
        jnp.dot(attended, out_weight, preferred_element_type=jnp.float32).astype(jnp.bfloat16), "tp"
    ).astype(jnp.float32)
    mixed = lax.dynamic_slice_in_dim(summed, lax.axis_index("tp") * rows_out, rows_out, 0).astype(
        jnp.bfloat16
    )
    gathered = lax.dot_general(
        lax.all_gather(out_grad, "tp", axis=0, tiled=True),
        out_weight,
        (((1,), (1,)), ((), ())),
        preferred_element_type=jnp.float32,
    )
    d_attended = gathered.astype(jnp.bfloat16)
    d_heads = d_attended.reshape(local_span_list, SPAN, heads_here, HD)
    d_prob = jnp.einsum("cqhd,ckhd->chqk", d_heads, value_rows, preferred_element_type=jnp.float32)
    row_dot = jnp.sum(attn_prob * d_prob, axis=-1, keepdims=True)
    d_scores = (attn_prob * (d_prob - row_dot)).astype(jnp.bfloat16)
    d_query = (
        jnp.einsum("chqk,ckhd->cqhd", d_scores, key_rows, preferred_element_type=jnp.float32)
        * score_scale
    )
    d_queries = d_query.astype(jnp.bfloat16).reshape(tokens_here, col_width)
    d_key = (
        jnp.einsum("chqk,cqhd->ckhd", d_scores, query_rows, preferred_element_type=jnp.float32)
        * score_scale
    )
    d_value = jnp.einsum("chqk,cqhd->ckhd", prob_b, d_heads, preferred_element_type=jnp.float32)
    d_key = d_key.reshape(local_span_list * NEIGH, BR * col_width)
    d_value = d_value.reshape(local_span_list * NEIGH, BR * col_width)
    slot_hits = (span_slots[None, :] == jnp.arange(slot_count)[:, None]).astype(jnp.float32)
    position_indices = jnp.dot(slot_hits, d_key, precision=lax.Precision.HIGHEST)
    slot_values = jnp.dot(slot_hits, d_value, precision=lax.Precision.HIGHEST)
    position_indices = position_indices.astype(jnp.bfloat16).reshape(seq_count, CAP, BR * col_width)
    slot_values = slot_values.astype(jnp.bfloat16).reshape(seq_count, CAP, BR * col_width)
    back_keys, back_values = (
        lax.all_to_all(position_indices, "seq", split_axis=0, concat_axis=0, tiled=True),
        lax.all_to_all(slot_values, "seq", split_axis=0, concat_axis=0, tiled=True),
    )
    back_keys = back_keys.reshape(slot_count, BR * col_width)
    back_values = back_values.reshape(slot_count, BR * col_width)
    unpack_dims = (((0,), (0,)), ((), ()))
    d_keys = lax.dot_general(select, back_keys, unpack_dims, preferred_element_type=jnp.float32)
    d_values = lax.dot_general(select, back_values, unpack_dims, preferred_element_type=jnp.float32)
    d_keys = d_keys.astype(jnp.bfloat16).reshape(blocks_here * BR, col_width)
    d_values = d_values.astype(jnp.bfloat16).reshape(blocks_here * BR, col_width)
    return (mixed, d_queries, d_keys, d_values)


def solution(mesh):
    placed = (
        P("seq", "tp"),
        P("seq", "tp"),
        P("seq", "tp"),
        P("tp", None),
        P(("seq", "tp"), None),
        P("seq", None),
        P("seq"),
        P("seq"),
    )
    return jax.shard_map(
        on_device,
        mesh=mesh,
        in_specs=placed,
        out_specs=(P(("seq", "tp"), None), P("seq", "tp"), P("seq", "tp"), P("seq", "tp")),
        check_vma=False,
    )
```

profile of v0, /device:TPU:0, one launch (start us, length us, event | category | flops | bytes accessed | tf_op | source)
XLA Modules:
  0.0 385.3 jit_solution(10135763885658955213)
XLA Ops:
  7.2 0.8 convert_reduce_fusion
  10.1 8.1 %all-to-all-start.1 = ((bf16[16,1,2]{2,1,0:T(2,128)(2,1)}), bf16[16,1,2]{2,1,0:T(2,128)(2,1)S(1)}, u32[]{:S(2)}, u32[]{:S(2)}) async-start(bf16[16,1,2]{2,1,0:T(2,128)(2,1)} %all_to_all.24), calls=%async_computation.1 | async-start | bytes 16384 | tf_op jit(solution)/shard_map/all_to_all | solution.py:47
  18.3 2.2 reshape.164
  20.5 3.2 convolution_convert_fusion.2
  23.7 5.9 %reshape.165 = bf16[16,2,65536]{2,1,0:T(2,128)(2,1)} reshape(bf16[32,65536]{1,0:T(8,128)(2,1)} %convolution_convert_fusion.2) | data formatting | bytes 8388608 | tf_op jit(solution)/shard_map/reshape | solution.py:38
  29.6 7.3 %all-to-all-start.2 = ((bf16[16,2,65536]{2,1,0:T(2,128)(2,1)}), bf16[16,2,65536]{2,1,0:T(2,128)(2,1)}, u32[]{:S(2)}, u32[]{:S(2)}) async-start(bf16[16,2,65536]{2,1,0:T(2,128)(2,1)} %reshape.165), calls=%async_computation.2 | async-start | bytes 8388608 | tf_op jit(solution)/shard_map/all_to_all | solution.py:45
  36.9 2.2 reshape.157
  39.1 3.2 convolution_convert_fusion.3
  42.3 5.9 %reshape.158 = bf16[16,2,65536]{2,1,0:T(2,128)(2,1)} reshape(bf16[32,65536]{1,0:T(8,128)(2,1)} %convolution_convert_fusion.3) | data formatting | bytes 8388608 | tf_op jit(solution)/shard_map/reshape | solution.py:38
  48.2 50.2 %all-to-all-done.2 = bf16[16,2,65536]{2,1,0:T(2,128)(2,1)} async-done(((bf16[16,2,65536]{2,1,0:T(2,128)(2,1)}), bf16[16,2,65536]{2,1,0:T(2,128)(2,1)}, u32[]{:S(2)}, u32[]{:S(2)}) %all-to-all-start.2) | async-done | bytes 4194336 | tf_op jit(solution)/shard_map/all_to_all | solution.py:45
  98.3 5.0 %all-to-all-start = ((bf16[16,2,65536]{2,1,0:T(2,128)(2,1)}), bf16[16,2,65536]{2,1,0:T(2,128)(2,1)}, u32[]{:S(2)}, u32[]{:S(2)}) async-start(bf16[16,2,65536]{2,1,0:T(2,128)(2,1)} %reshape.158), calls=%async_computation | async-start | bytes 8388608 | tf_op jit(solution)/shard_map/all_to_all | solution.py:46
  105.6 5.5 %reshape.166 = bf16[32,65536]{1,0:T(8,128)(2,1)} reshape(bf16[16,2,65536]{2,1,0:T(2,128)(2,1)} %all-to-all-done.2) | data formatting | bytes 8388608 | tf_op jit(solution)/shard_map/reshape | solution.py:49
  111.1 6.4 %gather_fusion.2 = bf16[16,65536]{1,0:T(8,128)(2,1)S(1)} fusion(bf16[32,65536]{1,0:T(8,128)(2,1)} %reshape.166, s32[1024]{0:T(1024)S(1)} %pad_clamp_fusion), kind=kCustom, calls=%fused_computation.1.clone | custom fusion | bytes 4194368 | tf_op jit(solution)/shard_map/jit(_take)/gather | solution.py:53
  117.5 44.1 %all-to-all-done = bf16[16,2,65536]{2,1,0:T(2,128)(2,1)} async-done(((bf16[16,2,65536]{2,1,0:T(2,128)(2,1)}), bf16[16,2,65536]{2,1,0:T(2,128)(2,1)}, u32[]{:S(2)}, u32[]{:S(2)}) %all-to-all-start) | async-done | bytes 4194336 | tf_op jit(solution)/shard_map/all_to_all | solution.py:46
  161.6 5.4 %reshape.159 = bf16[32,65536]{1,0:T(8,128)(2,1)} reshape(bf16[16,2,65536]{2,1,0:T(2,128)(2,1)} %all-to-all-done) | data formatting | bytes 8388608 | tf_op jit(solution)/shard_map/reshape | solution.py:50
  167.0 7.7 %gather_fusion.1 = bf16[16,65536]{1,0:T(8,128)(2,1)} fusion(bf16[32,65536]{1,0:T(8,128)(2,1)} %reshape.159, s32[1024]{0:T(1024)S(1)} %pad_clamp_fusion), kind=kCustom, calls=%fused_computation.clone | custom fusion | bytes 4194368 | tf_op jit(solution)/shard_map/jit(_take)/gather | solution.py:56
  174.7 4.0 %broadcast_select_fusion = (bf16[16,65536]{1,0:T(8,128)(2,1)}, bf16[16,65536]{1,0:T(8,128)(2,1)}) fusion(bf16[16,65536]{1,0:T(8,128)(2,1)S(1)} %gather_fusion.2, pred[16]{0:T(512)(128)(4,1)S(1)} %compare_and_fusion, bf16[16,65536]{1,0:T(8,128)(2,1)} %gather_fusion.1), kind=kLoop, calls=%fused_computation.22 | loop fusion | flops 2097152 | bytes 8388624 | tf_op jit(solution)/shard_map/jit(_take)/select_n | solution.py:53
  178.7 3.2 reshape.167
  182.0 0.8 fusion.12
  182.8 2.3 fusion.53
  185.1 11.1 %convolution_convert_fusion.7 = bf16[512,512]{1,0:T(8,128)(2,1)} fusion(bf16[512,8192]{1,0:T(8,128)(2,1)} %all-gather.2.cloned.1.call-done, bf16[512,8192]{1,0:T(8,128)(2,1)} %param.13), kind=kOutput, calls=%fused_computation.35 | convolution fusion | flops 4295229440 | bytes 17301504 | tf_op jit(solution)/shard_map/dot_general | solution.py:85
  196.2 1.2 reshape.170
  197.3 4.5 %convolution_bitcast_fusion = f32[8,256,4,128]{1,3,2,0:T(8,128)} fusion(bf16[8,64,4,128]{3,2,1,0:T(4,128)(2,1)S(1)} %reshape.170, f32[8,4,64,256]{3,2,1,0:T(8,128)} %get-tuple-element.8, f32[8,4,64]{2,1,0:T(4,128)S(1)} %get-tuple-element.7), kind=kOutput, calls=%fused_computation.12 | convolution fusion | flops 135266304 | bytes 6823936 | tf_op jit(solution)/shard_map/chqk,cqhd->ckhd/dot_general | solution.py:105
  201.8 5.2 %copy.81 = f32[8,256,4,128]{3,2,1,0:T(4,128)} copy(f32[8,256,4,128]{1,3,2,0:T(8,128)} %convolution_bitcast_fusion) | data formatting | bytes 8388608 | tf_op jit(solution)/shard_map/chqk,cqhd->ckhd/transpose | solution.py:105
  207.0 4.9 %reshape.176 = f32[16,65536]{1,0:T(8,128)} reshape(f32[8,256,4,128]{3,2,1,0:T(4,128)} %copy.81) | data formatting | bytes 8388608 | tf_op jit(solution)/shard_map/reshape | solution.py:107
  212.0 7.8 %convolution_convert_fusion = bf16[32,65536]{1,0:T(8,128)(2,1)} fusion(f32[16,65536]{1,0:T(8,128)} %reshape.176, s32[16]{0:T(128)S(1)} %reshape.160), kind=kOutput, calls=%fused_computation.4 | convolution fusion | flops 404750848 | bytes 8388672 | tf_op jit(solution)/shard_map/dot_general | solution.py:110
  219.7 5.9 %reshape.177 = bf16[16,2,65536]{2,1,0:T(2,128)(2,1)} reshape(bf16[32,65536]{1,0:T(8,128)(2,1)} %convolution_convert_fusion) | data formatting | bytes 8388608 | tf_op jit(solution)/shard_map/reshape | solution.py:112
  225.6 4.5 %all-to-all-start.4 = ((bf16[16,2,65536]{2,1,0:T(2,128)(2,1)}), bf16[16,2,65536]{2,1,0:T(2,128)(2,1)}, u32[]{:S(2)}, u32[]{:S(2)}) async-start(bf16[16,2,65536]{2,1,0:T(2,128)(2,1)} %reshape.177), calls=%async_computation.4 | async-start | bytes 8388608 | tf_op jit(solution)/shard_map/all_to_all | solution.py:115
  230.2 4.2 %reshape.161 = bf16[8,256,4,128]{3,2,1,0:T(4,128)(2,1)} reshape(bf16[16,65536]{1,0:T(8,128)(2,1)} %get-tuple-element.6) | data formatting | bytes 4194304 | tf_op jit(solution)/shard_map/reshape | solution.py:56
  234.5 2.8 fusion.26
  237.7 10.1 %convolution_convert_fusion.6 = bf16[512,8192]{1,0:T(8,128)(2,1)} fusion(bf16[512,8192]{1,0:T(8,128)(2,1)} %param.13, bf16[64,8,4,128]{3,2,1,0:T(4,128)(2,1)S(1)} %bitcast.57), kind=kOutput, calls=%fused_computation.10 | convolution fusion | flops 4299161600 | bytes 17301504 | tf_op jit(solution)/shard_map/dot_general | solution.py:80
  247.8 3.3 multiply_reduce_fusion
  251.8 1.0 copy-done
  253.6 4.9 %copy.79 = f32[8,256,4,128]{3,2,1,0:T(4,128)} copy(f32[8,256,4,128]{3,1,2,0:T(8,128)S(1)} %multiply_bitcast_fusion) | data formatting | bytes 8388608 | tf_op jit(solution)/shard_map/mul | solution.py:102
  258.5 4.9 %reshape.172 = f32[16,65536]{1,0:T(8,128)} reshape(f32[8,256,4,128]{3,2,1,0:T(4,128)} %copy.79) | data formatting | bytes 8388608 | tf_op jit(solution)/shard_map/reshape | solution.py:106
  263.4 7.9 %convolution_convert_fusion.1 = bf16[32,65536]{1,0:T(8,128)(2,1)} fusion(f32[16,65536]{1,0:T(8,128)} %reshape.172, s32[16]{0:T(128)S(1)} %reshape.160), kind=kOutput, calls=%fused_computation.5 | convolution fusion | flops 404750848 | bytes 8388672 | tf_op jit(solution)/shard_map/dot_general | solution.py:109
  271.2 6.2 %reshape.173 = bf16[16,2,65536]{2,1,0:T(2,128)(2,1)} reshape(bf16[32,65536]{1,0:T(8,128)(2,1)} %convolution_convert_fusion.1) | data formatting | bytes 8388608 | tf_op jit(solution)/shard_map/reshape | solution.py:111
  277.4 7.0 %all-to-all-done.4 = bf16[16,2,65536]{2,1,0:T(2,128)(2,1)} async-done(((bf16[16,2,65536]{2,1,0:T(2,128)(2,1)}), bf16[16,2,65536]{2,1,0:T(2,128)(2,1)}, u32[]{:S(2)}, u32[]{:S(2)}) %all-to-all-start.4) | async-done | bytes 4194336 | tf_op jit(solution)/shard_map/all_to_all | solution.py:115
  284.5 4.6 %all-to-all-start.3 = ((bf16[16,2,65536]{2,1,0:T(2,128)(2,1)}), bf16[16,2,65536]{2,1,0:T(2,128)(2,1)}, u32[]{:S(2)}, u32[]{:S(2)}) async-start(bf16[16,2,65536]{2,1,0:T(2,128)(2,1)} %reshape.173), calls=%async_computation.3 | async-start | bytes 8388608 | tf_op jit(solution)/shard_map/all_to_all | solution.py:114
  289.0 64.5 %all-reduce.2.cloned.1.call-done = bf16[512,8192]{1,0:T(8,128)(2,1)} async-done(((bf16[512,8192]{1,0:T(8,128)(2,1)}), bf16[512,8192]{1,0:T(8,128)(2,1)}) %all-reduce.2.cloned.1.call-update) | async-done | bytes 8388624 | tf_op jit(solution)/shard_map/psum | solution.py:79
  353.6 2.3 convert_convert_fusion
  356.7 0.9 copy.119
  357.6 5.4 %reshape.178 = bf16[32,65536]{1,0:T(8,128)(2,1)} reshape(bf16[16,2,65536]{2,1,0:T(2,128)(2,1)} %all-to-all-done.4) | data formatting | bytes 8388608 | tf_op jit(solution)/shard_map/reshape | solution.py:118
  363.0 2.9 convolution_convert_fusion.4
  365.9 2.0 reshape.179
  367.9 5.4 %reshape.174 = bf16[32,65536]{1,0:T(8,128)(2,1)} reshape(bf16[16,2,65536]{2,1,0:T(2,128)(2,1)} %all-to-all-done.3) | data formatting | bytes 8388608 | tf_op jit(solution)/shard_map/reshape | solution.py:117
  373.3 2.9 convolution_convert_fusion.5
  376.3 2.0 reshape.175
  (42 shorter events, 7.2 us)
Async XLA Ops:
  10.1 19.4 %all-to-all-start.1 = ((bf16[16,1,2]{2,1,0:T(2,128)(2,1)}), bf16[16,1,2]{2,1,0:T(2,128)(2,1)S(1)}, u32[]{:S(2)}, u32[]{:S(2)}) async-start(bf16[16,1,2]{2,1,0:T(2,128)(2,1)} %all_to_all.24), calls=%async_computation.1 | async-start | bytes 16384 | tf_op jit(solution)/shard_map/all_to_all | solution.py:47
  29.6 68.8 %all-to-all-start.2 = ((bf16[16,2,65536]{2,1,0:T(2,128)(2,1)}), bf16[16,2,65536]{2,1,0:T(2,128)(2,1)}, u32[]{:S(2)}, u32[]{:S(2)}) async-start(bf16[16,2,65536]{2,1,0:T(2,128)(2,1)} %reshape.165), calls=%async_computation.2 | async-start | bytes 8388608 | tf_op jit(solution)/shard_map/all_to_all | solution.py:45
  48.1 56.0 %copy-start.4 = (s32[8,2]{0,1:T(2,128)S(1)}, s32[8,2]{0,1:T(2,128)}, u32[]{:S(2)}) copy-start(s32[8,2]{0,1:T(2,128)} %param.15) | copy-start | bytes 196
  48.2 56.2 %copy-start.3 = (bf16[512,512]{1,0:T(8,128)(2,1)S(1)}, bf16[512,512]{1,0:T(8,128)(2,1)}, u32[]{:S(2)}) copy-start(bf16[512,512]{1,0:T(8,128)(2,1)} %param.10) | copy-start | bytes 1572868
  98.3 63.2 %all-to-all-start = ((bf16[16,2,65536]{2,1,0:T(2,128)(2,1)}), bf16[16,2,65536]{2,1,0:T(2,128)(2,1)}, u32[]{:S(2)}, u32[]{:S(2)}) async-start(bf16[16,2,65536]{2,1,0:T(2,128)(2,1)} %reshape.158), calls=%async_computation | async-start | bytes 8388608 | tf_op jit(solution)/shard_map/all_to_all | solution.py:46
  103.4 81.7 %all-gather.2.cloned.1.call-start = ((), (), s32[]{:S(2)}) async-start(), calls=%async_computation.6 | async-start | bytes 9437184 | tf_op jit(solution)/shard_map/all_gather | solution.py:86
  225.6 58.8 %all-to-all-start.4 = ((bf16[16,2,65536]{2,1,0:T(2,128)(2,1)}), bf16[16,2,65536]{2,1,0:T(2,128)(2,1)}, u32[]{:S(2)}, u32[]{:S(2)}) async-start(bf16[16,2,65536]{2,1,0:T(2,128)(2,1)} %reshape.177), calls=%async_computation.4 | async-start | bytes 8388608 | tf_op jit(solution)/shard_map/all_to_all | solution.py:115
  230.2 123.4 %all-reduce.2.cloned.1.call-start = ((), (), s32[]{:S(2)}) async-start(), calls=%async_computation.5 | async-start | bytes 16777216 | tf_op jit(solution)/shard_map/psum | solution.py:79
  247.8 3.3 copy-start.2
  251.8 1.0 copy-start
  284.5 83.4 %all-to-all-start.3 = ((bf16[16,2,65536]{2,1,0:T(2,128)(2,1)}), bf16[16,2,65536]{2,1,0:T(2,128)(2,1)}, u32[]{:S(2)}, u32[]{:S(2)}) async-start(bf16[16,2,65536]{2,1,0:T(2,128)(2,1)} %reshape.173), calls=%async_computation.3 | async-start | bytes 8388608 | tf_op jit(solution)/shard_map/all_to_all | solution.py:114
  289.0 66.8 %copy-start.1 = (bf16[8,4,64,256]{3,2,1,0:T(8,128)(2,1)S(1)}, bf16[8,4,64,256]{3,2,1,0:T(8,128)(2,1)}, u32[]{:S(2)}) copy-start(bf16[8,4,64,256]{3,2,1,0:T(8,128)(2,1)} %copy-done) | copy-start | bytes 3145732
Sparse Core Ops, SparseCore 0:
  105.9 51.1 all-gather.1
  247.9 105.6 all-reduce.1
where the time goes:
time: 392 us; the launch traced here: 385 us
  waiting for transfers between devices  166 us (42%)
  local copies, waits for them, and re-layouts  101 us (26%)
  matrix products  62.4 us (16%)
  starting transfers between devices  30.1 us (8%)
  between operations  14.6 us (4%)
  other arithmetic  10.9 us (3%)
    psum x1, waiting for transfers between devices, on_device(): lax.psum(jnp.dot(attended, out_weight, preferred_element_type=jnp.float32...  64.5 us
    all_to_all x1, waiting for transfers between devices, on_device(): lax.all_to_all(pack(nb_keys), 'seq', split_axis=0, concat_axis=0, tiled=T...  50.2 us
    all_to_all x1, waiting for transfers between devices, on_device(): lax.all_to_all(pack(nb_values), 'seq', split_axis=0, concat_axis=0, tiled...  44.1 us
    reshape x2, local copies, waits for them, and re-layouts, pack(): return packed.astype(jnp.bfloat16).reshape(seq_count, CAP, BR * col_width)  11.7 us
    dot_general x1, matrix products, on_device(): lax.dot_general(lax.all_gather(out_grad, 'tp', axis=0, tiled=True), out_w...  11.1 us
    dot_general x1, matrix products, on_device(): jnp.dot(attended, out_weight, preferred_element_type=jnp.float32)  10.1 us
    all_to_all x1, starting transfers between devices, on_device(): lax.all_to_all(sent_valid, 'seq', split_axis=0, concat_axis=0, tiled=True)  8.13 us
    dot_general x1, matrix products, on_device(): jnp.dot(slot_hits, d_key, precision=lax.Precision.HIGHEST)  7.85 us
  transfers between devices with their start and end apart: 7, of which 4 were waited for; matrix products, arithmetic and copies ran while one was open for 31% of the time, Pallas kernels for 0%

commit v1 on v0

v1 whole, which is shorter than its diff:
```python
import functools

import jax
import jax.numpy as jnp
from jax import lax
from jax.experimental import pallas as pl
from jax.experimental.pallas import tpu as pltpu
from jax.sharding import PartitionSpec as P

HD = 128
SPAN = 64
BR = 128
NEIGH = 2
CAP = 2
RING = 4
DEAD = 16.0
DEAD_EDGE = 12.0
NEG = -1e30
F32 = jnp.float32
BF16 = jnp.bfloat16
SMEM = pl.BlockSpec(memory_space=pltpu.SMEM)
VMEM = pl.BlockSpec(memory_space=pltpu.VMEM)
ANY = pl.BlockSpec(memory_space=pl.ANY)
NT = (((1,), (1,)), ((), ()))
NN = (((1,), (0,)), ((), ()))
TN = (((0,), (0,)), ((), ()))
MIB = 1 << 20
PLACE = 3


def dot(a, b, dims):
    return lax.dot_general(a, b, dims, preferred_element_type=F32)


def split_seq(meta, index):
    high, low = index // RING, index % RING
    first = meta[0] == 0
    return jnp.where(first, high, low), jnp.where(first, low, high)


def block_places(meta, blocks):
    dest = [meta[PLACE + j] for j in range(blocks)]
    places = []
    for j in range(blocks):
        rank = jnp.int32(0)
        for i in range(j):
            rank = rank + jnp.where(dest[i] == dest[j], 1, 0)
        to_a, to_b = split_seq(meta, dest[j])
        places.append(((to_a - meta[1] + RING) % RING, to_b * CAP + rank))
    return places


def pack_kernel(meta, keys, values, p0, p1, p2, p3, held, in_sem, out_sem):
    packed = (p0, p1, p2, p3)
    blocks = held.shape[1]
    per_ring = RING * CAP
    reads = [
        [pltpu.make_async_copy(src.at[j], held.at[t, j], in_sem.at[t, j]) for j in range(blocks)]
        for t, src in enumerate((keys, values))
    ]
    for j in range(blocks):
        reads[0][j].start()
        reads[1][j].start()
    places = block_places(meta, blocks)
    row = lax.broadcasted_iota(jnp.int32, (BR, HD), 0)
    for j, (shift, pos) in enumerate(places):
        reads[0][j].wait()
        first = held[0, j, :, :HD].astype(F32)
        valid = meta[PLACE + blocks + j]
        held[0, j, :, :HD] = jnp.where(row < valid, first, DEAD).astype(BF16)
        reads[1][j].wait()
        for d in range(RING):

            @pl.when(shift == d)
            def _():
                for t in range(2):
                    to = packed[d].at[pos + t * per_ring]
                    pltpu.make_async_copy(held.at[t, j], to, out_sem.at[t, j]).start()

    for j in range(blocks):
        for t in range(2):
            pltpu.make_async_copy(held.at[t, j], packed[0].at[0], out_sem.at[t, j]).wait()


def unpack_kernel(meta, p0, p1, p2, p3, d_keys, d_values, held, in_sem, out_sem):
    packed = (p0, p1, p2, p3)
    outs = (d_keys, d_values)
    blocks = d_keys.shape[0]
    per_ring = RING * CAP
    table = PLACE + 2 * blocks
    reads = []
    for d in range(RING):
        to = held.at[pl.ds(2 * d * per_ring, packed[d].shape[0])]
        reads.append(pltpu.make_async_copy(packed[d], to, in_sem.at[d]))
        reads[-1].start()
    empty = 2 * RING * per_ring
    held[empty] = jnp.zeros(held.shape[1:], BF16)
    kept = packed[1].shape[0] // 2
    writes = []
    places = block_places(meta, blocks)
    for read in reads:
        read.wait()
    for j, (shift, pos) in enumerate(places):
        back = meta[table + shift * per_ring + pos]
        half = jnp.where(shift == 0, per_ring, kept)
        for t in range(2):
            at = jnp.where(back < 0, empty, 2 * shift * per_ring + back + t * half)
            writes.append(pltpu.make_async_copy(held.at[at], outs[t].at[j], out_sem.at[t, j]))
            writes[-1].start()
    for write in writes:
        write.wait()


def locate(meta, spans, i, n):
    d = i // spans
    slot = meta[PLACE + i * NEIGH + n]
    from_a, from_b = split_seq(meta, slot // CAP)
    to_b = (meta[2] - d + RING) % RING
    block = (meta[1] - from_a + RING) % RING * (RING * CAP) + to_b * CAP + slot % CAP
    return block, from_b == meta[2]


def diagonal_reads(src, buf, d, spans, heads, sem):
    reads = []
    for h in range(heads):
        at = h % 2
        to = buf.at[
            pl.ds(d * spans, spans), h // 2, pl.ds(at * SPAN, SPAN), pl.ds(at * HD, HD)
        ]
        here = src.at[pl.ds(0, spans), :, pl.ds(h * HD, HD)]
        reads.append(pltpu.make_async_copy(here, to, sem.at[h]))
    return reads


def clear_others(buf):
    count = buf.shape[0]

    def one(i, _):
        for t in range(buf.shape[1]):
            buf[i, t, :SPAN, HD:] = jnp.zeros((SPAN, HD), BF16)
            buf[i, t, SPAN:, :HD] = jnp.zeros((SPAN, HD), BF16)
        return 0

    lax.fori_loop(0, count, one, 0)


def forward_kernel(heads, spans, *args):
    meta, queries, blocks_in, outs = args[0], args[1:5], args[5:9], args[9:13]
    q_buf, kv_buf, o_buf, s_buf, spans_at, counts, q_sem, sem = args[13:]
    tokens = spans * SPAN
    per_ring = RING * CAP
    twins = heads // 2
    reads = []
    for d in range(RING):
        reads += diagonal_reads(queries[d], q_buf, d, spans, heads, q_sem.at[d])
    block_reads = [
        pltpu.make_async_copy(blocks_in[d], kv_buf.at[d], sem.at[RING + d]) for d in range(RING)
    ]
    for copy in reads + block_reads:
        copy.start()
    for r in range(RING + 1):
        counts[r] = 0
    stride = 3 * (RING * spans + 1)

    def listed(i, _):
        block0, here0 = locate(meta, spans, i, 0)
        block1, here1 = locate(meta, spans, i, 1)
        first = jnp.where(here0, block0, block1)
        which = jnp.where(jnp.logical_and(here0, here1), RING, first // per_ring)
        at = which * stride + 3 * counts[which]
        spans_at[at] = i
        spans_at[at + 1] = first
        spans_at[at + 2] = block1
        counts[which] = counts[which] + jnp.where(jnp.logical_or(here0, here1), 1, 0)
        return 0

    lax.fori_loop(0, RING * spans, listed, 0)
    clear_others(q_buf)
    o_buf[:, :tokens, :] = jnp.zeros((RING, tokens, heads * HD), BF16)
    s_buf[...] = jnp.full(s_buf.shape, NEG, F32)
    for copy in reads:
        copy.wait()
    scale = HD ** (-0.5)

    def span(i, at):
        d, g = i // spans, i % spans
        rows = pl.ds(pl.multiple_of(g * SPAN, SPAN), SPAN)
        where = [(b // per_ring, b % per_ring) for b in at]
        live = [kv_buf[r, p, :, :HD][:, :1].astype(F32) < DEAD_EDGE for r, p in where]
        for t in range(twins):
            cols = slice(2 * t * HD, 2 * (t + 1) * HD)
            q = q_buf[i, t]
            scores = [
                jnp.where(here, dot(kv_buf[r, p, :, cols], q, NT) * scale, NEG)
                for here, (r, p) in zip(live, where)
            ]
            top = functools.reduce(jnp.maximum, [jnp.max(s, axis=0, keepdims=True) for s in scores])
            terms = [jnp.exp(s - top) for s in scores]
            total = sum(jnp.sum(e, axis=0, keepdims=True) for e in terms)
            share = 1.0 / total
            mixed = sum(
                dot((e * share).astype(BF16), kv_buf[r, per_ring + p, :, cols], TN)
                for e, (r, p) in zip(terms, where)
            ).astype(BF16)
            o_buf[d, rows, 2 * t * HD : (2 * t + 1) * HD] = mixed[:SPAN, :HD]
            o_buf[d, rows, (2 * t + 1) * HD : 2 * (t + 1) * HD] = mixed[SPAN:, HD:]
            s_buf[pl.ds(i * twins + t, 1), :] = top + jnp.log(total)

    for r in range(RING + 1):
        count = counts[r]

        def two(t, _):
            for u in range(2):
                at = r * stride + 3 * jnp.minimum(2 * t + u, count - 1)
                span(spans_at[at], [spans_at[at + 1 + n] for n in range(2 if r == RING else 1)])
            return 0

        if r < RING:
            block_reads[r].wait()
        lax.fori_loop(0, (count + 1) // 2, two, 0)

    out_copies = []
    rows_in = spans * twins
    for d in range(RING):
        part = s_buf[d * rows_in : (d + 1) * rows_in, :]
        for t in range(3):
            piece = part.astype(BF16)
            o_buf[d, tokens:, t * HD : (t + 1) * HD] = piece
            part = part - piece.astype(F32)
        out_copies.append(pltpu.make_async_copy(o_buf.at[d], outs[d], sem.at[d]))
        out_copies[-1].start()
    for copy in out_copies:
        copy.wait()


def merge_kernel(heads, *args):
    parts, d_att = args[0:4], args[4]
    out, stats_out, lse_buf = args[5:]
    tokens = out.shape[0]
    spans = tokens // SPAN
    twins = heads // 2
    stat_rows = spans * twins
    for d in range(RING):
        pieces = [parts[d][tokens:, t * HD : (t + 1) * HD].astype(F32) for t in range(3)]
        lse_buf[d] = pieces[0] + pieces[1] + pieces[2]
    top = functools.reduce(jnp.maximum, [lse_buf[d] for d in range(RING)])
    total = sum(jnp.exp(lse_buf[d] - top) for d in range(RING))
    whole = top + jnp.log(total)
    stats_out[:stat_rows, :] = whole
    for d in range(RING):
        lse_buf[d] = jnp.exp(lse_buf[d] - whole)
    token = lax.broadcasted_iota(jnp.int32, (SPAN, HD), 0)
    lane = lax.broadcasted_iota(jnp.int32, (SPAN, HD), 1)
    diagonal = (token == lane, token + SPAN == lane)

    def span(g, _):
        rows = pl.ds(pl.multiple_of(g * SPAN, SPAN), SPAN)
        for t in range(twins):
            row_dots = []
            for u in range(2):
                h = 2 * t + u
                cols = slice(h * HD, (h + 1) * HD)
                acc = jnp.zeros((SPAN, HD), F32)
                for d in range(RING):
                    row = lse_buf[d, pl.ds(g * twins + t, 1), :]
                    weight = jnp.sum(jnp.where(diagonal[u], row, 0.0), axis=1, keepdims=True)
                    acc += weight * parts[d][rows, cols].astype(F32)
                out[rows, cols] = acc.astype(BF16)
                row_dot = jnp.sum(acc * d_att[rows, cols].astype(F32), axis=1, keepdims=True)
                row_dots.append(jnp.where(diagonal[u], row_dot, 0.0))
            stats_out[pl.ds(stat_rows + g * twins + t, 1), :] = jnp.sum(
                row_dots[0] + row_dots[1], axis=0, keepdims=True
            )
        return 0

    lax.fori_loop(0, spans, span, 0)


def backward_kernel(heads, spans, *args):
    meta, queries, d_atts, blocks_in, stats = args[0], args[1:5], args[5:9], args[9:13], args[13:17]
    d_qs, d_blocks = args[17:21], args[21:25]
    q_buf, g_buf, kv_buf, s_buf, dq_buf, dq_acc, dk_acc, dv_acc = args[25:33]
    pairs, counts, seen, q_sem, g_sem, sem = args[33:]
    per_ring = RING * CAP
    twins = heads // 2
    stat_rows = spans * twins
    order = (1, 3, 2, 0)
    reads = []
    for d in range(RING):
        reads += diagonal_reads(queries[d], q_buf, d, spans, heads, q_sem.at[d])
        reads += diagonal_reads(d_atts[d], g_buf, d, spans, heads, g_sem.at[d])
        reads.append(pltpu.make_async_copy(stats[d], s_buf.at[d], sem.at[4 * d]))
    block_reads = [
        pltpu.make_async_copy(blocks_in[d], kv_buf.at[d], sem.at[4 * d + 3]) for d in range(RING)
    ]
    for copy in reads:
        copy.start()
    for r in order:
        block_reads[r].start()
    for r in range(RING):
        counts[r] = 0
    for b in range(RING * per_ring):
        seen[b] = 0
    stride = 2 * (RING * spans * NEIGH + 1)

    def listed(i, _):
        for n in range(NEIGH):
            block, here = locate(meta, spans, i, n)
            which = block // per_ring
            at = which * stride + 2 * counts[which]
            pairs[at] = i
            pairs[at + 1] = block % per_ring
            counts[which] = counts[which] + jnp.where(here, 1, 0)
            seen[block] = jnp.where(here, 1, seen[block])
        return 0

    lax.fori_loop(0, RING * spans, listed, 0)
    clear_others(q_buf)
    clear_others(g_buf)
    dq_acc[...] = jnp.zeros(dq_acc.shape, F32)
    for copy in reads:
        copy.wait()
    scale = HD ** (-0.5)
    writes = []
    for r in order:
        count = counts[r]

        def clear(p, _):
            @pl.when(seen[r * per_ring + p] == 1)
            def _():
                dk_acc[p] = jnp.zeros((BR, heads * HD), F32)
                dv_acc[p] = jnp.zeros((BR, heads * HD), F32)

            return 0

        def two(t, _):
            found = []
            for u in range(2):
                at = r * stride + 2 * jnp.minimum(2 * t + u, count - 1)
                i, p = pairs[at], pairs[at + 1]
                d, g = i // spans, i % spans
                live = kv_buf[r, p, :, :HD][:, :1].astype(F32) < DEAD_EDGE
                real = 2 * t + u < count
                to = (jnp.where(real, i, RING * spans), jnp.where(real, p, per_ring))
                for w in range(twins):
                    cols = slice(2 * w * HD, 2 * (w + 1) * HD)
                    q, g_att = q_buf[i, w], g_buf[i, w]
                    k = kv_buf[r, p, :, cols]
                    v = kv_buf[r, per_ring + p, :, cols]
                    lse = s_buf[d, pl.ds(g * twins + w, 1), :]
                    row_dot = s_buf[d, pl.ds(stat_rows + g * twins + w, 1), :]
                    prob = jnp.where(live, jnp.exp(dot(k, q, NT) * scale - lse), 0.0)
                    d_s = (prob * (dot(v, g_att, NT) - row_dot)).astype(BF16)
                    d_v, d_k = dot(prob.astype(BF16), g_att, NN), dot(d_s, q, NN)
                    found.append((to, w, d_v, d_k, dot(d_s, k, TN)))
            for (i, p), w, d_v, d_k, d_q in found:
                cols = slice(2 * w * HD, 2 * (w + 1) * HD)
                dv_acc[p, :, cols] += d_v
                dk_acc[p, :, cols] += d_k
                dq_acc[i, :, 2 * w * HD : (2 * w + 1) * HD] += d_q[:SPAN, :HD]
                dq_acc[i, :, (2 * w + 1) * HD : 2 * (w + 1) * HD] += d_q[SPAN:, HD:]
            return 0

        def finish(p, at):
            one = seen[r * per_ring + p]

            @pl.when(one == 1)
            def _():
                kv_buf[r, at] = (dk_acc[p] * scale).astype(BF16)
                kv_buf[r, d_blocks[r].shape[0] // 2 + at] = dv_acc[p].astype(BF16)

            return at + one

        lax.fori_loop(0, per_ring, clear, 0)
        block_reads[r].wait()
        lax.fori_loop(0, (count + 1) // 2, two, 0)
        lax.fori_loop(0, per_ring, finish, jnp.int32(0))
        here = kv_buf.at[r, pl.ds(0, d_blocks[r].shape[0])]
        writes.append(pltpu.make_async_copy(here, d_blocks[r], sem.at[4 * r + 3]))
        writes[-1].start()
    for d in range(RING):
        for g in range(spans):
            dq_buf[d, g] = (dq_acc[d * spans + g] * scale).astype(BF16)
        writes.append(pltpu.make_async_copy(dq_buf.at[d], d_qs[d], sem.at[4 * d + 1]))
        writes[-1].start()
    for write in writes:
        write.wait()


def call(kernel, outs, in_specs, out_specs, scratch, cost, *operands, vmem=58):
    return pl.pallas_call(
        kernel,
        out_shape=outs,
        in_specs=in_specs,
        out_specs=out_specs,
        scratch_shapes=scratch,
        compiler_params=pltpu.CompilerParams(vmem_limit_bytes=vmem * MIB),
        cost_estimate=pl.CostEstimate(flops=cost[0], bytes_accessed=cost[1], transcendentals=0),
    )(*operands)


def on_device(
    queries, nb_keys, nb_values, out_weight, out_grad, span_refs, block_dest, block_valid
):
    seq_count = lax.axis_size("seq")
    tp_count = lax.axis_size("tp")
    tokens, width = queries.shape
    heads = width // HD
    spans = tokens // SPAN
    blocks = block_dest.shape[0]
    per_ring = RING * CAP
    stat_rows = spans * heads // 2
    ref_count = spans * NEIGH
    dma = pltpu.SemaphoreType.DMA

    seq_at = lax.axis_index("seq")
    core = lax.axis_index("tp") % 2
    high, low = seq_at // RING, seq_at % RING
    place = jnp.stack(
        [core, jnp.where(core == 0, high, low), jnp.where(core == 0, low, high)]
    ).astype(jnp.int32)

    def ring_pairs(shift, along_a):
        pairs = []
        for s in range(seq_count):
            z, y = s // RING, s % RING
            for t in range(tp_count):
                if (t % 2 == 0) == along_a:
                    to = (z + shift) % RING * RING + y
                else:
                    to = z * RING + (y + shift) % RING
                pairs.append((s * tp_count + t, to * tp_count + t))
        return pairs

    def move(x, shift, along_a):
        return lax.ppermute(x, ("seq", "tp"), ring_pairs(shift % RING, along_a))

    order = (1, 3, 2)

    def spread(parts, along_a, sign):
        got = {0: parts[0]}
        for d in order:
            got[d] = move(parts[d], sign * d, along_a)
        return tuple(got[d] for d in range(RING))

    grad_rows = lax.all_gather(out_grad, "tp", axis=0, tiled=True)

    slot_count = seq_count * CAP
    ref_rows = jnp.pad(
        span_refs.astype(BF16).reshape(1, 1, ref_count),
        ((0, 0), (0, SPAN - 1), (0, width - ref_count)),
    )
    q_sent = jnp.concatenate([queries.reshape(spans, SPAN, width), ref_rows], axis=0)
    q_all = spread((q_sent,) * RING, False, 1)
    refs = jnp.concatenate([q[spans, 0, :ref_count] for q in q_all]).astype(jnp.int32)
    meta = jnp.concatenate([place, refs])
    pack_meta = jnp.concatenate([place, block_dest, block_valid])

    kv_shape = jax.ShapeDtypeStruct((2 * per_ring, BR, width), BF16)
    packed = call(
        pack_kernel,
        (kv_shape,) * RING,
        [SMEM, ANY, ANY],
        (ANY,) * RING,
        [
            pltpu.VMEM((2, blocks, BR, width), BF16),
            dma((2, blocks)),
            dma((2, blocks)),
        ],
        (0, 16 * MIB),
        pack_meta,
        nb_keys.reshape(blocks, BR, width),
        nb_values.reshape(blocks, BR, width),
    )
    kv_all = spread(packed, True, 1)

    d_attended = lax.dot_general(
        grad_rows, out_weight, (((1,), (1,)), ((), ())), preferred_element_type=F32
    ).astype(BF16)
    g_all = spread((d_attended.reshape(spans, SPAN, width),) * RING, False, 1)

    kv_now, q_now, d_attended = lax.optimization_barrier((kv_all, q_all, d_attended))
    twin_rows = (RING * spans, heads // 2, 2 * SPAN, 2 * HD)
    part_shape = jax.ShapeDtypeStruct((tokens + stat_rows, width), BF16)
    found = call(
        functools.partial(forward_kernel, heads, spans),
        (part_shape,) * RING,
        [SMEM] + [ANY] * 8,
        (ANY,) * RING,
        [
            pltpu.VMEM(twin_rows, BF16),
            pltpu.VMEM((RING, 2 * per_ring, BR, width), BF16),
            pltpu.VMEM((RING, tokens + stat_rows, width), BF16),
            pltpu.VMEM((RING * stat_rows, HD), F32),
            pltpu.SMEM((3 * (RING + 1) * (RING * spans + 1),), jnp.int32),
            pltpu.SMEM((RING + 1,), jnp.int32),
            dma((RING, heads)),
            dma((2 * RING,)),
        ],
        (10**11, 12 * MIB),
        meta,
        *q_now,
        *kv_now,
    )
    found, refs = lax.optimization_barrier((found, refs))
    parts = spread(found, False, -1)
    step = jnp.arange(RING)
    ring_b = (place[2] - step + RING) % RING
    owner = jnp.where(core == 0, place[1] * RING + ring_b, ring_b * RING + place[1])
    ring_keys = (owner[:, None] * slot_count + refs.reshape(RING, ref_count)).reshape(-1)
    all_keys = jnp.concatenate(spread((ring_keys.astype(jnp.int32),) * RING, True, 1))
    parts, all_keys = lax.optimization_barrier((parts, all_keys))
    span_shape = jax.ShapeDtypeStruct((spans, SPAN, width), BF16)
    rows_shape = jax.ShapeDtypeStruct((tokens, width), BF16)
    stat_shape = jax.ShapeDtypeStruct((2 * stat_rows, HD), F32)
    attended, stats = call(
        functools.partial(merge_kernel, heads),
        (rows_shape, stat_shape),
        [VMEM] * 5,
        (VMEM, VMEM),
        [pltpu.VMEM((RING, stat_rows, HD), F32)],
        (10**11, 4 * MIB),
        *parts,
        d_attended,
        vmem=40,
    )
    stats_all = spread((stats,) * RING, False, 1)
    attended, g_all = lax.optimization_barrier((attended, g_all))
    partial = jnp.dot(attended, out_weight, preferred_element_type=F32).astype(BF16)
    mixed = lax.psum_scatter(partial, "tp", scatter_dimension=0, tiled=True)

    named = jnp.any(all_keys[None, :] == jnp.arange(seq_count * slot_count)[:, None], axis=1)
    shape = (RING, RING, RING, RING, CAP)
    named = named.reshape(shape).astype(jnp.int32)
    other = (1 - jnp.eye(RING, dtype=jnp.int32))
    most = jnp.maximum(
        jnp.max(jnp.sum(named, axis=(1, 4)) * other[:, :, None]),
        jnp.max(jnp.sum(named, axis=(0, 4)) * other[:, None, :]),
    )
    to_a = (place[1] + step[:, None, None]) % RING
    to_b = step[None, :, None]
    owner = jnp.where(core == 0, to_a * RING + to_b, to_b * RING + to_a)
    sent = owner * slot_count + seq_at * CAP + jnp.arange(CAP)[None, None, :]
    sent = sent.reshape(RING, per_ring)
    sent_named = jnp.any(all_keys[None, None, :] == sent[:, :, None], axis=2).astype(jnp.int32)
    earlier = (jnp.arange(per_ring)[:, None] < jnp.arange(per_ring)[None, :]).astype(jnp.int32)
    position = jnp.sum(sent_named[:, :, None] * earlier[None], axis=1)
    position = jnp.where(sent_named == 1, position, -1).reshape(RING * per_ring)
    unpack_meta = jnp.concatenate([pack_meta, position])
    block_out = jax.ShapeDtypeStruct((blocks, BR, width), BF16)

    def backward(kept):
        back_shape = jax.ShapeDtypeStruct((2 * kept, BR, width), BF16)
        grads = call(
            functools.partial(backward_kernel, heads, spans),
            (span_shape,) * RING + (kv_shape,) + (back_shape,) * (RING - 1),
            [SMEM] + [ANY] * 16,
            (ANY,) * (2 * RING),
            [
                pltpu.VMEM(twin_rows, BF16),
                pltpu.VMEM(twin_rows, BF16),
                pltpu.VMEM((RING, 2 * per_ring, BR, width), BF16),
                pltpu.VMEM((RING,) + stat_shape.shape, F32),
                pltpu.VMEM((RING,) + span_shape.shape, BF16),
                pltpu.VMEM((RING * spans + 1, SPAN, width), F32),
                pltpu.VMEM((per_ring + 1, BR, width), F32),
                pltpu.VMEM((per_ring + 1, BR, width), F32),
                pltpu.SMEM((2 * RING * (RING * spans * NEIGH + 1),), jnp.int32),
                pltpu.SMEM((RING,), jnp.int32),
                pltpu.SMEM((RING * per_ring,), jnp.int32),
                dma((RING, heads)),
                dma((RING, heads)),
                dma((4 * RING,)),
            ],
            (10**11, 24 * MIB),
            meta,
            *q_now,
            *g_all,
            *kv_now,
            *stats_all,
        )
        back_blocks = spread(grads[RING:], True, -1)
        back_queries = spread(grads[:RING], False, -1)
        d_queries = sum(part.astype(F32) for part in back_queries).astype(BF16)
        d_queries = d_queries.reshape(tokens, width)
        return (d_queries,) + tuple(
            call(
                unpack_kernel,
                (block_out, block_out),
                [SMEM] + [ANY] * RING,
                (ANY, ANY),
                [
                    pltpu.VMEM((2 * RING * per_ring + 1, BR, width), BF16),
                    dma((RING,)),
                    dma((2, blocks)),
                ],
                (0, 16 * MIB),
                unpack_meta,
                *back_blocks,
            )
        )

    d_queries, d_keys, d_values = backward(per_ring)
    return (
        mixed,
        d_queries,
        d_keys.reshape(blocks * BR, width),
        d_values.reshape(blocks * BR, width),
    )


def solution(mesh):
    placed = (
        P("seq", "tp"),
        P("seq", "tp"),
        P("seq", "tp"),
        P("tp", None),
        P(("seq", "tp"), None),
        P("seq", None),
        P("seq"),
        P("seq"),
    )
    return jax.shard_map(
        on_device,
        mesh=mesh,
        in_specs=placed,
        out_specs=(P(("seq", "tp"), None), P("seq", "tp"), P("seq", "tp"), P("seq", "tp")),
        check_vma=False,
    )
```

time: 392 us -> 233 us (0.59); the launches traced: 385 us -> 232 us
  local copies, waits for them, and re-layouts: 101 us -> 4.41 us
  waiting for transfers between devices: 166 us -> 99.4 us
  matrix products: 62.4 us -> 17 us
  Pallas kernels: 0 us -> 44.2 us
  starting transfers between devices: 30.1 us -> 45.8 us
  other arithmetic: 10.9 us -> 6.61 us
    all_to_all x5 -> x0, waiting for transfers between devices: 101 us -> none  [the longest x1 50.2 us: on_device(): lax.all_to_all(pack(nb_keys), 'seq', split_axis=0, concat_axis=0, tiled=T...]
    ppermute x0 -> x24, waiting for transfers between devices: none -> 91 us  [move(): return lax.ppermute(x, ('seq', 'tp'), ring_pairs(shift % RING, along_a))]
    reshape x21 -> x1, local copies, waits for them, and re-layouts: 72.8 us -> 0.09 us  [on_device(): span_refs.astype(BF16).reshape(1, 1, ref_count)]
    psum x1 -> x0, waiting for transfers between devices: 64.5 us -> none  [on_device(): lax.psum(jnp.dot(attended, out_weight, preferred_element_type=jnp.float32...]
    ppermute x0 -> x24, starting transfers between devices: none -> 45.8 us  [move(): return lax.ppermute(x, ('seq', 'tp'), ring_pairs(shift % RING, along_a))]
    dot_general x15 -> x2, matrix products: 62.4 us -> 17 us  [the longest x1 10.3 us: on_device(): lax.dot_general(grad_rows, out_weight, (((1,), (1,)), ((), ())), preferre...]
    pallas_call x0 -> x5, Pallas kernels: none -> 44.2 us  [call(): pl.pallas_call(kernel, out_shape=outs, in_specs=in_specs, out_specs=out_s...]
    all_to_all x5 -> x0, starting transfers between devices: 29.5 us -> none  [the longest x1 8.13 us: on_device(): lax.all_to_all(sent_valid, 'seq', split_axis=0, concat_axis=0, tiled=True)]
  transfers between devices with their start and end apart: 7 -> 26, of which waited for: 4 -> 15; matrix products, arithmetic and copies ran while one was open for 31% -> 8% of each run, Pallas kernels for 0% -> 14%
where the time goes in v1:
time: 233 us; the launch traced here: 232 us
  waiting for transfers between devices  99.4 us (43%)
  starting transfers between devices  45.8 us (20%)
  Pallas kernels  44.2 us (19%)
  matrix products  17 us (7%)
  between operations  14.3 us (6%)
  other arithmetic  6.61 us (3%)
  local copies, waits for them, and re-layouts  4.41 us (2%)
    ppermute x24, waiting for transfers between devices, move(): return lax.ppermute(x, ('seq', 'tp'), ring_pairs(shift % RING, along_a))  91 us
    ppermute x24, starting transfers between devices, move(): return lax.ppermute(x, ('seq', 'tp'), ring_pairs(shift % RING, along_a))  45.8 us
    pallas_call x5, Pallas kernels, call(): pl.pallas_call(kernel, out_shape=outs, in_specs=in_specs, out_specs=out_s...  44.2 us
    dot_general x1, matrix products, on_device(): lax.dot_general(grad_rows, out_weight, (((1,), (1,)), ((), ())), preferre...  10.3 us
    all_gather x1, waiting for transfers between devices, on_device(): grad_rows = lax.all_gather(out_grad, 'tp', axis=0, tiled=True)  7.65 us
    dot_general x1, matrix products, on_device(): jnp.dot(attended, out_weight, preferred_element_type=F32).astype(BF16)  6.71 us
  transfers between devices with their start and end apart: 26, of which 15 were waited for; matrix products, arithmetic and copies ran while one was open for 8% of the time, Pallas kernels for 14%

profile of v1, /device:TPU:0, one launch (start us, length us, event | category | flops | bytes accessed | tf_op | source)
XLA Modules:
  0.0 231.7 jit_solution(8323104032022321522)
XLA Ops:
  7.2 0.7 all-gather.2.cloned.1.call-update
  8.0 0.7 convert_element_type.45
  8.8 1.1 fusion.1.args_1_
  9.9 3.2 %collective-permute-start.2 = (bf16[9,64,512]{2,1,0:T(8,128)(2,1)S(1)}, bf16[9,64,512]{2,1,0:T(8,128)(2,1)S(1)}, u32[]{:S(2)}, u32[]{:S(2)}) collective-permute-start(bf16[9,64,512]{2,1,0:T(8,128)(2,1)S(1)} %fusion.1.args_1_), channel_id=1, source_target_pairs={{0,24},{1,97},{2,26},{3,99},{4,28},{5,101},{6,30},{7,103},{8,0},{9... | collective-permute-start | bytes 1769480 | tf_op jit(solution)/shard_map/ppermute | solution.py:436
  13.1 0.6 collective-permute-start.1
  13.7 1.0 collective-permute-start
  15.3 5.1 %shard_map.111 = (bf16[16,128,512]{2,1,0:T(8,128)(2,1)}, bf16[16,128,512]{2,1,0:T(8,128)(2,1)}, bf16[16,128,512]{2,1,0:T(8,128)(2,1)}, bf16[16,128,512]{2,1,0:T(8,128)(2,1)}) custom-call(s32[35]{0:T(128)} %concatenate.24.meta, bf16[16,128,512]{2,1,0:T(8,128)(2,1)} %bitcast.25, bf16[16,128,512]{2,1,0:T(8,128)(2,1)} %bitcast.26), custom_call_target="tpu_custom_call" | custom-call | bytes 16777216 | tf_op jit(solution)/shard_map/pallas_call | solution.py:391
  20.4 2.0 collective-permute-start.3
  22.4 3.6 %collective-permute-start.4 = (bf16[16,128,512]{2,1,0:T(8,128)(2,1)}, bf16[16,128,512]{2,1,0:T(8,128)(2,1)}, u32[]{:S(2)}, u32[]{:S(2)}) collective-permute-start(bf16[16,128,512]{2,1,0:T(8,128)(2,1)} %get-tuple-element.50), channel_id=1, source_target_pairs={{0,64},{1,17},{2,66},{3,19},{4,68},{5,21},{6,70},{7,23},{8,72},{9,... | collective-permute-start | bytes 6291464 | tf_op jit(solution)/shard_map/ppermute | solution.py:436
  26.1 23.3 %collective-permute-done.2.args_4_ = bf16[9,64,512]{2,1,0:T(8,128)(2,1)S(1)} collective-permute-done((bf16[9,64,512]{2,1,0:T(8,128)(2,1)S(1)}, bf16[9,64,512]{2,1,0:T(8,128)(2,1)S(1)}, u32[]{:S(2)}, u32[]{:S(2)}) %collective-permute-start.2) | collective-permute-done | bytes 589856 | tf_op jit(solution)/shard_map/ppermute | solution.py:436
  49.3 4.0 %collective-permute-start.5 = (bf16[16,128,512]{2,1,0:T(8,128)(2,1)}, bf16[16,128,512]{2,1,0:T(8,128)(2,1)}, u32[]{:S(2)}, u32[]{:S(2)}) collective-permute-start(bf16[16,128,512]{2,1,0:T(8,128)(2,1)} %get-tuple-element.51), channel_id=1, source_target_pairs={{0,96},{1,25},{2,98},{3,27},{4,100},{5,29},{6,102},{7,31},{8,104},... | collective-permute-start | bytes 6291464 | tf_op jit(solution)/shard_map/ppermute | solution.py:436
  53.5 0.8 pad_add_fusion.1.args_0_
  54.3 7.6 %all-gather.2.cloned.1.call-done = bf16[512,8192]{1,0:T(8,128)(2,1)} async-done(((bf16[64,8192]{1,0:T(8,128)(2,1)}), bf16[512,8192]{1,0:T(8,128)(2,1)}) %all-gather.2.cloned.1.call-update) | async-done | bytes 8388624 | tf_op jit(solution)/shard_map/all_gather | solution.py:446
  61.9 10.3 %convolution_convert_fusion.1.args_4_ = bf16[512,512]{1,0:T(8,128)(2,1)S(1)} fusion(bf16[512,8192]{1,0:T(8,128)(2,1)} %all-gather.2.cloned.1.call-done, bf16[512,8192]{1,0:T(8,128)(2,1)} %param.11), kind=kOutput, calls=%fused_computation.1 | convolution fusion | flops 4295229440 | bytes 17301504 | tf_op jit(solution)/shard_map/dot_general | solution.py:477
  72.3 3.3 %collective-permute-done.4.args_7_.args_11_ = bf16[16,128,512]{2,1,0:T(8,128)(2,1)} collective-permute-done((bf16[16,128,512]{2,1,0:T(8,128)(2,1)}, bf16[16,128,512]{2,1,0:T(8,128)(2,1)}, u32[]{:S(2)}, u32[]{:S(2)}) %collective-permute-start.4) | collective-permute-done | bytes 2097184 | tf_op jit(solution)/shard_map/ppermute | solution.py:436
  75.5 1.7 collective-permute-done.5.args_8_.args_12_
  77.2 11.0 %shard_map.112 = (bf16[528,512]{1,0:T(8,128)(2,1)}, bf16[528,512]{1,0:T(8,128)(2,1)}, bf16[528,512]{1,0:T(8,128)(2,1)}, bf16[528,512]{1,0:T(8,128)(2,1)}) custom-call(s32[67]{0:T(128)} %pad_add_fusion.1.args_0_, bf16[9,64,512]{2,1,0:T(8,128)(2,1)} %copy-done.4, bf16[9,64,512]{2,1,0:T(8,128)(2,1)} %copy-done.14, bf16[9,64,512]{2,1,0:T(8,128)(2,1)} %copy-done.13, ...), custom_call_target="tpu_custom_call" | custom-call | flops 99999997952 | bytes 12582912 | tf_op jit(solution)/shard_map/pallas_call | solution.py:391
  88.3 4.5 %collective-permute-start.6 = (bf16[528,512]{1,0:T(8,128)(2,1)}, bf16[528,512]{1,0:T(8,128)(2,1)S(1)}, u32[]{:S(2)}, u32[]{:S(2)}) collective-permute-start(bf16[528,512]{1,0:T(8,128)(2,1)} %get-tuple-element.65), channel_id=1, source_target_pairs={{0,24},{1,97},{2,26},{3,99},{4,28},{5,101},{6,30},{7,103},{8,0},{9... | collective-permute-start | bytes 1622024 | tf_op jit(solution)/shard_map/ppermute | solution.py:436
  92.8 0.9 collective-permute-start.8
  94.5 1.1 collective-permute-start.11
  95.5 2.9 %collective-permute-start.10 = (s32[64]{0:T(128)S(1)}, s32[64]{0:T(128)S(1)}, u32[]{:S(2)}, u32[]{:S(2)}) collective-permute-start(s32[64]{0:T(128)S(1)} %add.175), channel_id=1, source_target_pairs={{0,64},{1,17},{2,66},{3,19},{4,68},{5,21},{6,70},{7,23},{8,72},{9,... | collective-permute-start | bytes 776 | tf_op jit(solution)/shard_map/ppermute | solution.py:436
  98.4 1.3 collective-permute-start.9
  99.7 1.0 collective-permute-done.10
  100.7 2.7 %collective-permute-start.14 = (bf16[8,64,512]{2,1,0:T(8,128)(2,1)S(1)}, bf16[8,64,512]{2,1,0:T(8,128)(2,1)S(1)}, u32[]{:S(2)}, u32[]{:S(2)}) collective-permute-start(bf16[8,64,512]{2,1,0:T(8,128)(2,1)S(1)} %bitcast.21), channel_id=1, source_target_pairs={{0,24},{1,97},{2,26},{3,99},{4,28},{5,101},{6,30},{7,103},{8,0},{9... | collective-permute-start | bytes 1572872 | tf_op jit(solution)/shard_map/ppermute | solution.py:436
  103.4 3.2 %collective-permute-done.9 = s32[64]{0:T(128)S(1)} collective-permute-done((s32[64]{0:T(128)S(1)}, s32[64]{0:T(128)S(1)}, u32[]{:S(2)}, u32[]{:S(2)}) %collective-permute-start.9) | collective-permute-done | bytes 288 | tf_op jit(solution)/shard_map/ppermute | solution.py:436
  107.0 0.6 pad_add_fusion
  107.6 3.3 %collective-permute-start.12 = (bf16[8,64,512]{2,1,0:T(8,128)(2,1)S(1)}, bf16[8,64,512]{2,1,0:T(8,128)(2,1)S(1)}, u32[]{:S(2)}, u32[]{:S(2)}) collective-permute-start(bf16[8,64,512]{2,1,0:T(8,128)(2,1)S(1)} %bitcast.23), channel_id=1, source_target_pairs={{0,8},{1,33},{2,10},{3,35},{4,12},{5,37},{6,14},{7,39},{8,16},{9,4... | collective-permute-start | bytes 1572872 | tf_op jit(solution)/shard_map/ppermute | solution.py:436
  110.9 1.0 copy-done.2
  111.9 2.7 %shard_map.113 = (bf16[512,512]{1,0:T(8,128)(2,1)S(1)}, f32[32,128]{1,0:T(8,128)S(1)}) custom-call(bf16[528,512]{1,0:T(8,128)(2,1)S(1)} %copy-done.2, bf16[528,512]{1,0:T(8,128)(2,1)S(1)} %collective-permute-done.6.args_1_, bf16[528,512]{1,0:T(8,128)(2,1)S(1)} %collective-permute-done.7.args_2_, bf16[528,512]{1,0:T(8,128)(2,1)S(1)} %collective-permute-done.8.args_3_, ...), custom_call_target="tpu_custom_call" | custom-call | flops 99999997952 | bytes 4194304 | tf_op jit(solution)/shard_map/pallas_call | solution.py:391
  114.6 2.3 collective-permute-done.14.args_8_
  117.3 5.5 %collective-permute-done.12.args_6_ = bf16[8,64,512]{2,1,0:T(8,128)(2,1)S(1)} collective-permute-done((bf16[8,64,512]{2,1,0:T(8,128)(2,1)S(1)}, bf16[8,64,512]{2,1,0:T(8,128)(2,1)S(1)}, u32[]{:S(2)}, u32[]{:S(2)}) %collective-permute-start.12) | collective-permute-done | bytes 524320 | tf_op jit(solution)/shard_map/ppermute | solution.py:436
  122.8 0.8 copy-done.17
  123.6 6.7 %convolution_convert_fusion = bf16[512,8192]{1,0:T(8,128)(2,1)} fusion(bf16[512,512]{1,0:T(8,128)(2,1)S(1)} %get-tuple-element.75, bf16[512,8192]{1,0:T(8,128)(2,1)S(1)} %copy-done.11), kind=kOutput, calls=%fused_computation | convolution fusion | flops 4299161600 | bytes 17301504 | tf_op jit(solution)/shard_map/dot_general | solution.py:529
  130.4 0.7 collective-permute-start.17
  131.5 1.0 collective-permute-start.15
  132.5 1.7 collective-permute-done.17.args_16_
  134.2 2.1 collective-permute-done.16.args_15_
  137.5 19.0 %shard_map.114 = (bf16[8,64,512]{2,1,0:T(8,128)(2,1)}, bf16[8,64,512]{2,1,0:T(8,128)(2,1)}, bf16[8,64,512]{2,1,0:T(8,128)(2,1)}, bf16[8,64,512]{2,1,0:T(8,128)(2...) custom-call(s32[67]{0:T(128)} %pad_add_fusion.1.args_0_, ...), custom_call_target="tpu_custom_call" | custom-call | flops 99999997952 | bytes 25165824 | tf_op jit(solution)/shard_map/pallas_call | solution.py:391
  156.6 5.2 %collective-permute-start.21 = (bf16[16,128,512]{2,1,0:T(8,128)(2,1)}, bf16[16,128,512]{2,1,0:T(8,128)(2,1)S(1)}, u32[]{:S(2)}, u32[]{:S(2)}) collective-permute-start(bf16[16,128,512]{2,1,0:T(8,128)(2,1)} %get-tuple-element.87), channel_id=1, source_target_pairs={{0,96},{1,25},{2,98},{3,27},{4,100},{5,29},{6,102},{7,31},{8,104},... | collective-permute-start | bytes 6291464 | tf_op jit(solution)/shard_map/ppermute | solution.py:436
  161.7 0.9 collective-permute-start.23
  162.8 1.4 collective-permute-start.18
  164.4 2.3 collective-permute-start.19
  166.7 11.1 %collective-permute-done.18 = bf16[8,64,512]{2,1,0:T(8,128)(2,1)S(1)} collective-permute-done((bf16[8,64,512]{2,1,0:T(8,128)(2,1)}, bf16[8,64,512]{2,1,0:T(8,128)(2,1)S(1)}, u32[]{:S(2)}, u32[]{:S(2)}) %collective-permute-start.18) | collective-permute-done | bytes 524320 | tf_op jit(solution)/shard_map/ppermute | solution.py:436
  177.8 2.4 %collective-permute-start.20 = (bf16[8,64,512]{2,1,0:T(8,128)(2,1)}, bf16[8,64,512]{2,1,0:T(8,128)(2,1)}, u32[]{:S(2)}, u32[]{:S(2)}) collective-permute-start(bf16[8,64,512]{2,1,0:T(8,128)(2,1)} %get-tuple-element.84), channel_id=1, source_target_pairs={{0,8},{1,33},{2,10},{3,35},{4,12},{5,37},{6,14},{7,39},{8,16},{9,4... | collective-permute-start | bytes 1572872 | tf_op jit(solution)/shard_map/ppermute | solution.py:436
  181.2 15.8 %collective-permute-done.20 = bf16[8,64,512]{2,1,0:T(8,128)(2,1)} collective-permute-done((bf16[8,64,512]{2,1,0:T(8,128)(2,1)}, bf16[8,64,512]{2,1,0:T(8,128)(2,1)}, u32[]{:S(2)}, u32[]{:S(2)}) %collective-permute-start.20) | collective-permute-done | bytes 524320 | tf_op jit(solution)/shard_map/ppermute | solution.py:436
  197.1 2.3 add_convert_fusion
  199.3 19.1 %collective-permute-done.23.p3 = bf16[16,128,512]{2,1,0:T(8,128)(2,1)} collective-permute-done((bf16[16,128,512]{2,1,0:T(8,128)(2,1)}, bf16[16,128,512]{2,1,0:T(8,128)(2,1)}, u32[]{:S(2)}, u32[]{:S(2)}) %collective-permute-start.23) | collective-permute-done | bytes 2097184 | tf_op jit(solution)/shard_map/ppermute | solution.py:436
  218.4 6.4 %shard_map.115 = (bf16[16,128,512]{2,1,0:T(8,128)(2,1)}, bf16[16,128,512]{2,1,0:T(8,128)(2,1)}) custom-call(s32[67]{0:T(128)} %concatenate.26.meta, bf16[16,128,512]{2,1,0:T(8,128)(2,1)} %get-tuple-element.86.p0, bf16[16,128,512]{2,1,0:T(8,128)(2,1)} %copy-done.3, bf16[16,128,512]{2,1,0:T(8,128)(2,1)} %collective-permute-done.22.p2, ...), custom_call_target="tpu_custom_call" | custom-call | bytes 16777216 | tf_op jit(solution)/shard_map/pallas_call | solution.py:391
  (86 shorter events, 5.6 us)
Async XLA Ops:
  7.2 7.6 %copy-start.8 = (s32[16]{0:T(128)S(1)}, s32[16]{0:T(128)}, u32[]{:S(2)}) copy-start(s32[16]{0:T(128)} %param.15) | copy-start | bytes 196
  7.2 7.5 %copy-start.6 = (s32[16]{0:T(128)S(1)}, s32[16]{0:T(128)}, u32[]{:S(2)}) copy-start(s32[16]{0:T(128)} %param.14) | copy-start | bytes 196
  7.2 54.7 %all-gather.2.cloned.1.call-start = ((), (), s32[]{:S(2)}) async-start(), calls=%async_computation.1 | async-start | bytes 9437184 | tf_op jit(solution)/shard_map/all_gather | solution.py:446
  7.9 216.9 %reduce-scatter.2.cloned.1.call-start = ((), (), s32[]{:S(2)}) async-start(), calls=%async_computation.2 | async-start | bytes 9437184 | tf_op jit(solution)/shard_map/reduce_scatter | solution.py:530
  9.9 10.4 %copy-start.4 = (bf16[9,64,512]{2,1,0:T(8,128)(2,1)}, bf16[9,64,512]{2,1,0:T(8,128)(2,1)S(1)}, u32[]{:S(2)}) copy-start(bf16[9,64,512]{2,1,0:T(8,128)(2,1)S(1)} %fusion.1.args_1_) | copy-start | bytes 1769476
  9.9 39.4 %collective-permute-start.2 = (bf16[9,64,512]{2,1,0:T(8,128)(2,1)S(1)}, bf16[9,64,512]{2,1,0:T(8,128)(2,1)S(1)}, u32[]{:S(2)}, u32[]{:S(2)}) collective-permute-start(bf16[9,64,512]{2,1,0:T(8,128)(2,1)S(1)} %fusion.1.args_1_), channel_id=1, source_target_pairs={{0,24},{1,97},{2,26},{3,99},{4,28},{5,101},{6,30},{7,103},{8,0},{9... | collective-permute-start | bytes 1769480 | tf_op jit(solution)/shard_map/ppermute | solution.py:436
  13.1 40.2 %collective-permute-start.1 = (bf16[9,64,512]{2,1,0:T(8,128)(2,1)S(1)}, bf16[9,64,512]{2,1,0:T(8,128)(2,1)S(1)}, u32[]{:S(2)}, u32[]{:S(2)}) collective-permute-start(bf16[9,64,512]{2,1,0:T(8,128)(2,1)S(1)} %fusion.1.args_1_), channel_id=1, source_target_pairs={{0,16},{1,65},{2,18},{3,67},{4,20},{5,69},{6,22},{7,71},{8,24},{9,... | collective-permute-start | bytes 1769480 | tf_op jit(solution)/shard_map/ppermute | solution.py:436
  13.7 39.6 %collective-permute-start = (bf16[9,64,512]{2,1,0:T(8,128)(2,1)S(1)}, bf16[9,64,512]{2,1,0:T(8,128)(2,1)S(1)}, u32[]{:S(2)}, u32[]{:S(2)}) collective-permute-start(bf16[9,64,512]{2,1,0:T(8,128)(2,1)S(1)} %fusion.1.args_1_), channel_id=1, source_target_pairs={{0,8},{1,33},{2,10},{3,35},{4,12},{5,37},{6,14},{7,39},{8,16},{9,4... | collective-permute-start | bytes 1769480 | tf_op jit(solution)/shard_map/ppermute | solution.py:436
  20.4 51.9 %collective-permute-start.3 = (bf16[16,128,512]{2,1,0:T(8,128)(2,1)}, bf16[16,128,512]{2,1,0:T(8,128)(2,1)}, u32[]{:S(2)}, u32[]{:S(2)}) collective-permute-start(bf16[16,128,512]{2,1,0:T(8,128)(2,1)} %get-tuple-element.49), channel_id=1, source_target_pairs={{0,32},{1,9},{2,34},{3,11},{4,36},{5,13},{6,38},{7,15},{8,40},{9,1... | collective-permute-start | bytes 6291464 | tf_op jit(solution)/shard_map/ppermute | solution.py:436
  22.4 53.1 %collective-permute-start.4 = (bf16[16,128,512]{2,1,0:T(8,128)(2,1)}, bf16[16,128,512]{2,1,0:T(8,128)(2,1)}, u32[]{:S(2)}, u32[]{:S(2)}) collective-permute-start(bf16[16,128,512]{2,1,0:T(8,128)(2,1)} %get-tuple-element.50), channel_id=1, source_target_pairs={{0,64},{1,17},{2,66},{3,19},{4,68},{5,21},{6,70},{7,23},{8,72},{9,... | collective-permute-start | bytes 6291464 | tf_op jit(solution)/shard_map/ppermute | solution.py:436
  49.3 22.9 %copy-start.12 = (bf16[9,64,512]{2,1,0:T(8,128)(2,1)}, bf16[9,64,512]{2,1,0:T(8,128)(2,1)S(1)}, u32[]{:S(2)}) copy-start(bf16[9,64,512]{2,1,0:T(8,128)(2,1)S(1)} %collective-permute-done.2.args_4_) | copy-start | bytes 1769476
  49.3 27.9 %collective-permute-start.5 = (bf16[16,128,512]{2,1,0:T(8,128)(2,1)}, bf16[16,128,512]{2,1,0:T(8,128)(2,1)}, u32[]{:S(2)}, u32[]{:S(2)}) collective-permute-start(bf16[16,128,512]{2,1,0:T(8,128)(2,1)} %get-tuple-element.51), channel_id=1, source_target_pairs={{0,96},{1,25},{2,98},{3,27},{4,100},{5,29},{6,102},{7,31},{8,104},... | collective-permute-start | bytes 6291464 | tf_op jit(solution)/shard_map/ppermute | solution.py:436
  53.4 18.9 %copy-start.13 = (bf16[9,64,512]{2,1,0:T(8,128)(2,1)}, bf16[9,64,512]{2,1,0:T(8,128)(2,1)S(1)}, u32[]{:S(2)}) copy-start(bf16[9,64,512]{2,1,0:T(8,128)(2,1)S(1)} %collective-permute-done.1.args_3_) | copy-start | bytes 1769476
  53.4 18.9 %copy-start.14 = (bf16[9,64,512]{2,1,0:T(8,128)(2,1)}, bf16[9,64,512]{2,1,0:T(8,128)(2,1)S(1)}, u32[]{:S(2)}) copy-start(bf16[9,64,512]{2,1,0:T(8,128)(2,1)S(1)} %collective-permute-done.args_2_) | copy-start | bytes 1769476
  72.2 38.6 %copy-start = (bf16[512,512]{1,0:T(8,128)(2,1)}, bf16[512,512]{1,0:T(8,128)(2,1)S(1)}, u32[]{:S(2)}) copy-start(bf16[512,512]{1,0:T(8,128)(2,1)S(1)} %convolution_convert_fusion.1.args_4_) | copy-start | bytes 1572868
  88.3 19.4 %collective-permute-start.6 = (bf16[528,512]{1,0:T(8,128)(2,1)}, bf16[528,512]{1,0:T(8,128)(2,1)S(1)}, u32[]{:S(2)}, u32[]{:S(2)}) collective-permute-start(bf16[528,512]{1,0:T(8,128)(2,1)} %get-tuple-element.65), channel_id=1, source_target_pairs={{0,24},{1,97},{2,26},{3,99},{4,28},{5,101},{6,30},{7,103},{8,0},{9... | collective-permute-start | bytes 1622024 | tf_op jit(solution)/shard_map/ppermute | solution.py:436
  92.8 18.1 %collective-permute-start.7 = (bf16[528,512]{1,0:T(8,128)(2,1)}, bf16[528,512]{1,0:T(8,128)(2,1)S(1)}, u32[]{:S(2)}, u32[]{:S(2)}) collective-permute-start(bf16[528,512]{1,0:T(8,128)(2,1)} %get-tuple-element.66), channel_id=1, source_target_pairs={{0,16},{1,65},{2,18},{3,67},{4,20},{5,69},{6,22},{7,71},{8,24},{9,... | collective-permute-start | bytes 1622024 | tf_op jit(solution)/shard_map/ppermute | solution.py:436
  92.8 18.1 %collective-permute-start.8 = (bf16[528,512]{1,0:T(8,128)(2,1)}, bf16[528,512]{1,0:T(8,128)(2,1)S(1)}, u32[]{:S(2)}, u32[]{:S(2)}) collective-permute-start(bf16[528,512]{1,0:T(8,128)(2,1)} %get-tuple-element.67), channel_id=1, source_target_pairs={{0,8},{1,33},{2,10},{3,35},{4,12},{5,37},{6,14},{7,39},{8,16},{9,4... | collective-permute-start | bytes 1622024 | tf_op jit(solution)/shard_map/ppermute | solution.py:436
  94.5 4.0 %collective-permute-start.11 = (s32[64]{0:T(128)S(1)}, s32[64]{0:T(128)S(1)}, u32[]{:S(2)}, u32[]{:S(2)}) collective-permute-start(s32[64]{0:T(128)S(1)} %add.175), channel_id=1, source_target_pairs={{0,96},{1,25},{2,98},{3,27},{4,100},{5,29},{6,102},{7,31},{8,104},... | collective-permute-start | bytes 776 | tf_op jit(solution)/shard_map/ppermute | solution.py:436
  95.5 5.2 %collective-permute-start.10 = (s32[64]{0:T(128)S(1)}, s32[64]{0:T(128)S(1)}, u32[]{:S(2)}, u32[]{:S(2)}) collective-permute-start(s32[64]{0:T(128)S(1)} %add.175), channel_id=1, source_target_pairs={{0,64},{1,17},{2,66},{3,19},{4,68},{5,21},{6,70},{7,23},{8,72},{9,... | collective-permute-start | bytes 776 | tf_op jit(solution)/shard_map/ppermute | solution.py:436
  98.4 8.1 %collective-permute-start.9 = (s32[64]{0:T(128)S(1)}, s32[64]{0:T(128)S(1)}, u32[]{:S(2)}, u32[]{:S(2)}) collective-permute-start(s32[64]{0:T(128)S(1)} %add.175), channel_id=1, source_target_pairs={{0,32},{1,9},{2,34},{3,11},{4,36},{5,13},{6,38},{7,15},{8,40},{9,1... | collective-permute-start | bytes 776 | tf_op jit(solution)/shard_map/ppermute | solution.py:436
  100.7 16.3 %collective-permute-start.14 = (bf16[8,64,512]{2,1,0:T(8,128)(2,1)S(1)}, bf16[8,64,512]{2,1,0:T(8,128)(2,1)S(1)}, u32[]{:S(2)}, u32[]{:S(2)}) collective-permute-start(bf16[8,64,512]{2,1,0:T(8,128)(2,1)S(1)} %bitcast.21), channel_id=1, source_target_pairs={{0,24},{1,97},{2,26},{3,99},{4,28},{5,101},{6,30},{7,103},{8,0},{9... | collective-permute-start | bytes 1572872 | tf_op jit(solution)/shard_map/ppermute | solution.py:436
  106.5 10.8 %collective-permute-start.13 = (bf16[8,64,512]{2,1,0:T(8,128)(2,1)S(1)}, bf16[8,64,512]{2,1,0:T(8,128)(2,1)S(1)}, u32[]{:S(2)}, u32[]{:S(2)}) collective-permute-start(bf16[8,64,512]{2,1,0:T(8,128)(2,1)S(1)} %bitcast.22), channel_id=1, source_target_pairs={{0,16},{1,65},{2,18},{3,67},{4,20},{5,69},{6,22},{7,71},{8,24},{9,... | collective-permute-start | bytes 1572872 | tf_op jit(solution)/shard_map/ppermute | solution.py:436
  107.6 15.2 %collective-permute-start.12 = (bf16[8,64,512]{2,1,0:T(8,128)(2,1)S(1)}, bf16[8,64,512]{2,1,0:T(8,128)(2,1)S(1)}, u32[]{:S(2)}, u32[]{:S(2)}) collective-permute-start(bf16[8,64,512]{2,1,0:T(8,128)(2,1)S(1)} %bitcast.23), channel_id=1, source_target_pairs={{0,8},{1,33},{2,10},{3,35},{4,12},{5,37},{6,14},{7,39},{8,16},{9,4... | collective-permute-start | bytes 1572872 | tf_op jit(solution)/shard_map/ppermute | solution.py:436
  110.9 1.1 copy-start.2
  111.9 11.7 %copy-start.11 = (bf16[512,8192]{1,0:T(8,128)(2,1)S(1)}, bf16[512,8192]{1,0:T(8,128)(2,1)}, u32[]{:S(2)}) copy-start(bf16[512,8192]{1,0:T(8,128)(2,1)} %param.11) | copy-start | bytes 25165828
  114.6 16.9 %copy-start.1 = (f32[32,128]{1,0:T(8,128)}, f32[32,128]{1,0:T(8,128)S(1)}, u32[]{:S(2)}) copy-start(f32[32,128]{1,0:T(8,128)S(1)} %get-tuple-element.80.args_13_) | copy-start | bytes 49156
  117.0 13.4 %copy-start.15 = (bf16[8,64,512]{2,1,0:T(8,128)(2,1)}, bf16[8,64,512]{2,1,0:T(8,128)(2,1)S(1)}, u32[]{:S(2)}) copy-start(bf16[8,64,512]{2,1,0:T(8,128)(2,1)S(1)} %collective-permute-done.14.args_8_) | copy-start | bytes 1572868
  117.3 13.0 %copy-start.16 = (bf16[8,64,512]{2,1,0:T(8,128)(2,1)}, bf16[8,64,512]{2,1,0:T(8,128)(2,1)S(1)}, u32[]{:S(2)}) copy-start(bf16[8,64,512]{2,1,0:T(8,128)(2,1)S(1)} %collective-permute-done.13.args_7_) | copy-start | bytes 1572868
  122.8 0.8 copy-start.17
  130.4 33.8 %copy-start.10 = (s32[4]{0:T(128)S(1)}, s32[4]{0:T(128)}, u32[]{:S(2)}) copy-start(s32[4]{0:T(128)} %get-tuple-element.92) | copy-start | bytes 52
  130.4 49.9 %copy-start.5 = (s32[256]{0:T(256)S(1)}, s32[256]{0:T(256)}, u32[]{:S(2)}) copy-start(s32[256]{0:T(256)} %pad_add_fusion) | copy-start | bytes 3076
  130.4 50.3 %copy-start.7 = (s32[16]{0:T(128)S(1)}, s32[16]{0:T(128)}, u32[]{:S(2)}) copy-start(s32[16]{0:T(128)} %param.14) | copy-start | bytes 196
  130.4 50.2 %copy-start.9 = (s32[16]{0:T(128)S(1)}, s32[16]{0:T(128)}, u32[]{:S(2)}) copy-start(s32[16]{0:T(128)} %param.15) | copy-start | bytes 196
  130.4 3.8 %collective-permute-start.17 = (f32[32,128]{1,0:T(8,128)S(1)}, f32[32,128]{1,0:T(8,128)S(1)}, u32[]{:S(2)}, u32[]{:S(2)}) collective-permute-start(f32[32,128]{1,0:T(8,128)S(1)} %get-tuple-element.80.args_13_), channel_id=1, source_target_pairs={{0,24},{1,97},{2,26},{3,99},{4,28},{5,101},{6,30},{7,103},{8,0},{9... | collective-permute-start | bytes 49160 | tf_op jit(solution)/shard_map/ppermute | solution.py:436
  131.1 5.2 %collective-permute-start.16 = (f32[32,128]{1,0:T(8,128)S(1)}, f32[32,128]{1,0:T(8,128)S(1)}, u32[]{:S(2)}, u32[]{:S(2)}) collective-permute-start(f32[32,128]{1,0:T(8,128)S(1)} %get-tuple-element.80.args_13_), channel_id=1, source_target_pairs={{0,16},{1,65},{2,18},{3,67},{4,20},{5,69},{6,22},{7,71},{8,24},{9,... | collective-permute-start | bytes 49160 | tf_op jit(solution)/shard_map/ppermute | solution.py:436
  131.5 5.4 %collective-permute-start.15 = (f32[32,128]{1,0:T(8,128)S(1)}, f32[32,128]{1,0:T(8,128)S(1)}, u32[]{:S(2)}, u32[]{:S(2)}) collective-permute-start(f32[32,128]{1,0:T(8,128)S(1)} %get-tuple-element.80.args_13_), channel_id=1, source_target_pairs={{0,8},{1,33},{2,10},{3,35},{4,12},{5,37},{6,14},{7,39},{8,16},{9,4... | collective-permute-start | bytes 49160 | tf_op jit(solution)/shard_map/ppermute | solution.py:436
  134.2 2.7 %copy-start.18 = (f32[32,128]{1,0:T(8,128)}, f32[32,128]{1,0:T(8,128)S(1)}, u32[]{:S(2)}) copy-start(f32[32,128]{1,0:T(8,128)S(1)} %collective-permute-done.17.args_16_) | copy-start | bytes 49156
  136.3 0.6 copy-start.19
  136.9 0.6 copy-start.20
  156.6 42.8 %collective-permute-start.21 = (bf16[16,128,512]{2,1,0:T(8,128)(2,1)}, bf16[16,128,512]{2,1,0:T(8,128)(2,1)S(1)}, u32[]{:S(2)}, u32[]{:S(2)}) collective-permute-start(bf16[16,128,512]{2,1,0:T(8,128)(2,1)} %get-tuple-element.87), channel_id=1, source_target_pairs={{0,96},{1,25},{2,98},{3,27},{4,100},{5,29},{6,102},{7,31},{8,104},... | collective-permute-start | bytes 6291464 | tf_op jit(solution)/shard_map/ppermute | solution.py:436
  161.7 37.6 %collective-permute-start.22 = (bf16[16,128,512]{2,1,0:T(8,128)(2,1)}, bf16[16,128,512]{2,1,0:T(8,128)(2,1)}, u32[]{:S(2)}, u32[]{:S(2)}) collective-permute-start(bf16[16,128,512]{2,1,0:T(8,128)(2,1)} %get-tuple-element.88), channel_id=1, source_target_pairs={{0,64},{1,17},{2,66},{3,19},{4,68},{5,21},{6,70},{7,23},{8,72},{9,... | collective-permute-start | bytes 6291464 | tf_op jit(solution)/shard_map/ppermute | solution.py:436
  161.7 56.7 %collective-permute-start.23 = (bf16[16,128,512]{2,1,0:T(8,128)(2,1)}, bf16[16,128,512]{2,1,0:T(8,128)(2,1)}, u32[]{:S(2)}, u32[]{:S(2)}) collective-permute-start(bf16[16,128,512]{2,1,0:T(8,128)(2,1)} %get-tuple-element.89), channel_id=1, source_target_pairs={{0,32},{1,9},{2,34},{3,11},{4,36},{5,13},{6,38},{7,15},{8,40},{9,1... | collective-permute-start | bytes 6291464 | tf_op jit(solution)/shard_map/ppermute | solution.py:436
  162.8 15.1 %collective-permute-start.18 = (bf16[8,64,512]{2,1,0:T(8,128)(2,1)}, bf16[8,64,512]{2,1,0:T(8,128)(2,1)S(1)}, u32[]{:S(2)}, u32[]{:S(2)}) collective-permute-start(bf16[8,64,512]{2,1,0:T(8,128)(2,1)} %get-tuple-element.82), channel_id=1, source_target_pairs={{0,24},{1,97},{2,26},{3,99},{4,28},{5,101},{6,30},{7,103},{8,0},{9... | collective-permute-start | bytes 1572872 | tf_op jit(solution)/shard_map/ppermute | solution.py:436
  164.4 16.8 %collective-permute-start.19 = (bf16[8,64,512]{2,1,0:T(8,128)(2,1)}, bf16[8,64,512]{2,1,0:T(8,128)(2,1)S(1)}, u32[]{:S(2)}, u32[]{:S(2)}) collective-permute-start(bf16[8,64,512]{2,1,0:T(8,128)(2,1)} %get-tuple-element.83), channel_id=1, source_target_pairs={{0,16},{1,65},{2,18},{3,67},{4,20},{5,69},{6,22},{7,71},{8,24},{9,... | collective-permute-start | bytes 1572872 | tf_op jit(solution)/shard_map/ppermute | solution.py:436
  177.8 19.2 %collective-permute-start.20 = (bf16[8,64,512]{2,1,0:T(8,128)(2,1)}, bf16[8,64,512]{2,1,0:T(8,128)(2,1)}, u32[]{:S(2)}, u32[]{:S(2)}) collective-permute-start(bf16[8,64,512]{2,1,0:T(8,128)(2,1)} %get-tuple-element.84), channel_id=1, source_target_pairs={{0,8},{1,33},{2,10},{3,35},{4,12},{5,37},{6,14},{7,39},{8,16},{9,4... | collective-permute-start | bytes 1572872 | tf_op jit(solution)/shard_map/ppermute | solution.py:436
  199.3 19.1 %copy-start.3 = (bf16[16,128,512]{2,1,0:T(8,128)(2,1)}, bf16[16,128,512]{2,1,0:T(8,128)(2,1)S(1)}, u32[]{:S(2)}) copy-start(bf16[16,128,512]{2,1,0:T(8,128)(2,1)S(1)} %collective-permute-done.21.p1) | copy-start | bytes 6291460
Sparse Core Ops, SparseCore 0:
  9.7 52.1 all-gather.1
  130.5 50.8 reduce-scatter.1
